TPU v7x, 128 devices: a whole 4x4x4 slice. The times are simulated.
128 devices in a mesh: basis: 16 (over z, y_hi, core), aux: 8 (over x, y_lo).
Axes of the slice: x: 4, y: 4 (y_hi: 2, y_lo: 2; y = y_hi * 2 + y_lo), z: 4, core: 2. Of those that a mesh axis runs over, the one named last changes fastest.
Arguments:
- three_index: bfloat16 [1536, 16, 8192], P('aux', None, 'basis'), may hold values from -0.47851562 to 0.47851562
Outputs:
- exchange: float32 [8192, 8192], P(('basis', 'aux'))
All inputs are finite; a program needn't handle non-finite values.
Results may differ from a plain program's by a relative error of at most 0.0003.
Values may be sent and summed in bfloat16 or wider, within the bound.
A program may use at most 192 MiB of HBM per device.

v0:
```python
import jax
import jax.numpy as jnp
from jax import lax
from jax.sharding import PartitionSpec as P


def contract(left, right):
    return lax.dot_general(
        left, right, (((0,), (0,)), ((), ())), preferred_element_type=jnp.float32
    )


def shards(three_index):
    aux_rows = three_index.shape[0] * three_index.shape[1]
    block = three_index.shape[2]
    own = three_index.reshape(aux_rows, block)
    piece = lax.all_gather(three_index, "basis", axis=2, tiled=True)
    row_block = contract(own, piece.reshape(aux_rows, piece.shape[2]))
    result = lax.psum_scatter(row_block, "aux", scatter_dimension=0, tiled=True)
    return result


def solution(mesh):
    return jax.shard_map(
        shards,
        mesh=mesh,
        in_specs=(P("aux", None, "basis"),),
        out_specs=P(("basis", "aux"), None),
        check_vma=False,
    )
```

profile of v0, /device:TPU:1, one launch (start us, length us, event | category | flops | bytes accessed | tf_op | source)
XLA Modules:
  0.0 688.4 jit_solution(4972234939270112364)
XLA Ops:
  6.5 0.0 all-gather.2.cloned.1.call-start
  6.5 5.3 copy.2
  11.8 0.0 all-gather.2.cloned.1.call-update
  11.8 0.0 reduce-scatter.2.cloned.1.call-start
  11.9 291.6 %all-gather.2.cloned.1.call-done = bf16[192,16,8192]{2,0,1:T(8,128)(2,1)} async-done(((bf16[192,16,512]{2,0,1:T(8,128)(2,1)}), bf16[192,16,8192]{2,0,1:T(8,128)(2,1)}) %all-gather.2.cloned.1.call-update) | async-done | bytes 50331664 | tf_op jit(solution)/shard_map/all_gather | solution.py:17
  303.5 54.8 %fusion.2 = f32[512,8192]{1,0:T(8,128)} fusion(bf16[192,16,512]{2,1,0:T(8,128)(2,1)} %param.1, bf16[192,16,8192]{2,0,1:T(8,128)(2,1)} %all-gather.2.cloned.1.call-done), kind=kOutput, calls=%fused_computation.2 | convolution fusion | flops 25769803776 | bytes 70254592 | tf_op jit(solution)/shard_map/dot_general | solution.py:8
  358.3 0.0 reduce-scatter.2.cloned.1.call-update
  358.3 323.2 %reduce-scatter.2.cloned.1.call-done = f32[64,8192]{1,0:T(8,128)} async-done(((f32[512,8192]{1,0:T(8,128)}), f32[64,8192]{1,0:T(8,128)}) %reduce-scatter.2.cloned.1.call-update) | async-done | bytes 2097168 | tf_op jit(solution)/shard_map/reduce_scatter | solution.py:19
Async XLA Ops:
  6.5 297.0 %all-gather.2.cloned.1.call-start = ((), (), s32[]{:S(2)}) async-start(), calls=%async_computation.1 | async-start | bytes 53477376 | tf_op jit(solution)/shard_map/all_gather | solution.py:17
  11.8 669.8 %reduce-scatter.2.cloned.1.call-start = ((), (), s32[]{:S(2)}) async-start(), calls=%async_computation.2 | async-start | bytes 18874368 | tf_op jit(solution)/shard_map/reduce_scatter | solution.py:19
Sparse Core Ops, SparseCore 0:
  11.9 291.5 all-gather.1
  358.5 323.0 reduce-scatter.1
where the time goes:
time: 689 us; the launch traced here: 688 us
  waiting for transfers between devices  615 us (89%)
  matrix products  54.8 us (8%)
  between operations  13.4 us (2%)
    reduce_scatter x1, waiting for transfers between devices, shards(): result = lax.psum_scatter(row_block, 'aux', scatter_dimension=0, tiled=True)  323 us
    all_gather x1, waiting for transfers between devices, shards(): piece = lax.all_gather(three_index, 'basis', axis=2, tiled=True)  292 us
    dot_general x1, matrix products, contract(): lax.dot_general(left, right, (((0,), (0,)), ((), ())), preferred_element_...  54.8 us
  transfers between devices with their start and end apart: 2, of which 2 were waited for; matrix products, arithmetic and copies ran while one was open for 0% of the time, Pallas kernels for 0%

commit v1 on v0

v1 whole, which is shorter than its diff:
```python
import jax
import jax.numpy as jnp
from jax import lax
from jax.experimental import pallas as pl
from jax.experimental.pallas import tpu as pltpu
from jax.sharding import PartitionSpec as P

MESH = pl.DeviceIdType.MESH


def position():
    b = lax.axis_index("basis")
    a = lax.axis_index("aux")
    return b // 4, (b // 2) % 2, b % 2, a // 2, a % 2


def device(z, h, c, x, l):
    return (z * 4 + h * 2 + c, x * 2 + l)


def remote(src, dst, send, recv, who):
    return pltpu.make_async_remote_copy(
        src_ref=src, dst_ref=dst, send_sem=send, recv_sem=recv,
        device_id=who, device_id_type=MESH,
    )


def kernel(a_ref, out_ref, stage, rows, cols, part, got1, got2, done, turned, byrow, bycol,
           ls, ss, rs, s1, r1, s2, r2, sr, rr, st, rt):
    z, h, c, x, l = position()
    m = 1 - l
    mate = device(z, h, c, x, m)
    other = device(z, 1 - h, c, x, m)
    cross = device(z, 1 - h, c, x, l)
    core = device(z, h, 1 - c, x, l)
    down = device((z + 3) % 4, h, c, x, l)
    up = device((z + 1) % 4, h, c, x, l)
    far = device((z + 2) % 4, h, c, x, l)
    xa = x + 1 - 2 * (x % 2)
    xb = 3 - x
    xo = 3 - xa
    near_a = device(z, h, c, xa, l)
    near_b = device(z, h, c, xb, l)
    depth = a_ref.shape[0]
    half = rows.shape[3]
    quarter = depth // 4

    barrier = pltpu.get_barrier_semaphore()
    senders = [mate, other, cross, core, up, near_a, near_b]
    for i in (1, 2):
        for cs in range(2):
            for xs in range(4):
                senders.append(device((z + 4 - i) % 4, h, cs, xs, l))
    for who in senders:
        pl.semaphore_signal(barrier, inc=1, device_id=who, device_id_type=MESH)

    loads = [
        pltpu.make_async_copy(
            a_ref.at[pl.ds(q * quarter, quarter)], stage.at[pl.ds(q * quarter, quarter)], ls.at[q]
        )
        for q in range(4)
    ]
    for one in loads:
        one.start()
    for q in range(4):
        loads[q].wait()

        def sort(n, carry):
            at = pl.multiple_of(q * quarter + n * 128, 128)
            block = stage[pl.ds(at, 128), :]
            for g in range(2):
                rows[0, g, pl.ds(at, 128), :] = jnp.concatenate(
                    [block[:, t * 128 + g * 64 : t * 128 + g * 64 + 64] for t in range(4)], axis=1
                )
            return carry

        lax.fori_loop(0, quarter // 128, sort, 0)
    pl.semaphore_wait(barrier, len(senders))

    def copy(n, src, dst, who):
        return remote(src, dst, ss.at[n], rs.at[n], who)

    mate1 = copy(0, rows.at[0, m], rows.at[1, m], mate)
    mate2 = copy(1, rows.at[0, l], rows.at[1, l], mate)
    relay2 = copy(2, rows.at[3, m], rows.at[2, m], mate)
    other1 = copy(3, rows.at[0, l], rows.at[3, l], other)
    relay1 = copy(4, rows.at[1, l], rows.at[2, l], other)
    other2 = copy(5, rows.at[0, m], rows.at[3, m], other)
    down1 = copy(6, rows.at[0, l], cols.at[2 + l, 0], down)
    down2 = copy(7, rows.at[1, l], cols.at[2 + m, 0], down)
    take = ((z + 2) % 4) // 2
    far1 = copy(8, rows.at[(take + l) % 2, l], cols.at[4, 0], far)
    core1 = copy(9, rows.at[0, l], cols.at[l, 1], core)
    core2 = copy(10, rows.at[1, l], cols.at[m, 1], core)
    core3 = copy(11, cols.at[2 + l, 0], cols.at[2 + l, 1], core)
    core4 = copy(12, cols.at[2 + m, 0], cols.at[2 + m, 1], core)
    core5 = copy(13, cols.at[4, 0], cols.at[4, 1], core)
    keep1 = pltpu.make_async_copy(rows.at[0, l], cols.at[l, 0], ls.at[4])
    keep2 = pltpu.make_async_copy(rows.at[1, l], cols.at[m, 0], ls.at[5])

    def multiply(i, hr, role, g, column, first):
        def body(cr, carry):
            block = lax.dot_general(
                rows[role, g], cols[column, cr], (((0,), (0,)), ((), ())),
                preferred_element_type=jnp.float32,
            ).reshape(4, 64, half)
            if first:
                part[i, hr, g, cr] = block
            else:
                part[i, hr, g, cr] += block
            return carry

        lax.fori_loop(0, 2, body, 0)

    def scatter1(i, hr, g):
        return [
            remote(
                part.at[i, hr, g, cr, piece], got1.at[i, hr, g, cr, k],
                s1.at[i, hr, g, cr, k], r1.at[i, hr, g, cr, k], near,
            )
            for cr, near, mine in ((0, near_a, xa), (1, near_b, xb))
            for k, piece in ((0, mine), (1, xo))
        ]

    def scatter2(i, hr, g):
        return [
            remote(
                part.at[i, hr, g, cr, piece], got2.at[i, hr, g, cr],
                s2.at[i, hr, g, cr], r2.at[i, hr, g, cr], near,
            )
            for cr, near, piece in ((0, near_b, xb), (1, near_a, xa))
        ]

    def begin(i, hr, g):
        for one in scatter1(i, hr, g):
            one.start()

    def middle(i, hr, g):
        for one in scatter1(i, hr, g):
            one.wait_recv()
        part[i, hr, g, 0, xb] += got1[i, hr, g, 0, 1]
        part[i, hr, g, 1, xa] += got1[i, hr, g, 1, 1]
        for one in scatter2(i, hr, g):
            one.start()

    def finish(i, hr, g):
        for one in scatter2(i, hr, g):
            one.wait_recv()
        for cr in range(2):
            done[i, hr, cr, pl.ds(pl.multiple_of(g * 64, 64), 64), :] = (
                part[i, hr, g, cr, x] + got1[i, hr, g, cr, 0] + got2[i, hr, g, cr]
            )

    def rowwise(i, hr, g, who):
        return remote(
            done.at[i, hr, :, pl.ds(pl.multiple_of(g * 64, 64), 64), :], byrow.at[hr, l, i],
            sr.at[i, hr, g], rr.at[i, hr, l], who,
        )

    def colwise(i, hr):
        return [
            remote(
                turned.at[i - 1, hr, cr, pl.ds(xs * 64, 64)], bycol.at[i - 1, hr, c, x],
                st.at[i - 1, hr, cr, xs], rt.at[i - 1, hr, c, x],
                device((z + i) % 4, h, (c + cr) % 2, xs, l),
            )
            for cr in range(2)
            for xs in range(4)
        ]

    def turn(i, hr):
        for cr in range(2):
            turned[i - 1, hr, cr] = done[i, hr, cr].T
        for one in colwise(i, hr):
            one.start()

    late = (z // 2 + l) % 2

    mate1.start()
    other1.start()
    down1.start()
    core1.start()
    keep1.start()

    @pl.when(take == l)
    def _():
        far1.start()

    keep1.wait()
    core1.wait_recv()
    multiply(0, 0, 0, l, l, True)
    multiply(0, 0, 0, m, l, True)

    mate1.wait_recv()
    down2.start()
    core2.start()
    keep2.start()
    mate1.wait_send()
    mate2.start()
    other1.wait_send()
    relay1.start()

    @pl.when(take != l)
    def _():
        far1.start()

    keep2.wait()
    core2.wait_recv()
    multiply(0, 0, 1, l, m, False)
    begin(0, 0, l)
    other1.wait_recv()
    multiply(0, 1, 3, m, m, True)
    down1.wait_recv()
    core3.start()
    core3.wait_recv()
    multiply(1, 0, 0, l, 2 + l, True)
    multiply(1, 0, 0, m, 2 + l, True)
    middle(0, 0, l)

    mate2.wait_send()
    relay2.start()
    relay1.wait_send()
    other2.start()
    mate2.wait_recv()
    multiply(0, 0, 1, m, m, False)
    begin(0, 0, m)
    relay1.wait_recv()
    multiply(0, 1, 2, m, l, False)
    begin(0, 1, m)
    multiply(1, 1, 2, m, 2 + l, True)
    finish(0, 0, l)
    middle(0, 0, m)
    middle(0, 1, m)
    down2.wait_recv()
    core4.start()
    core4.wait_recv()
    multiply(1, 0, 1, l, 2 + m, False)
    begin(1, 0, l)
    multiply(1, 0, 1, m, 2 + m, False)
    begin(1, 0, m)
    multiply(1, 1, 3, m, 2 + m, False)
    begin(1, 1, m)
    finish(0, 0, m)
    finish(0, 1, m)
    middle(1, 0, l)
    far1.wait_recv()
    core5.start()
    middle(1, 0, m)
    core5.wait_recv()
    multiply(2, 0, late, l, 4, True)
    begin(2, 0, l)
    multiply(2, 0, late, m, 4, True)
    begin(2, 0, m)
    multiply(2, 1, 2 + late, m, 4, True)
    begin(2, 1, m)
    middle(1, 1, m)
    finish(1, 0, l)
    finish(1, 0, m)
    turn(1, 0)

    other2.wait_recv()
    relay2.wait_recv()
    multiply(1, 1, 3, l, 2 + m, True)
    multiply(1, 1, 2, l, 2 + l, False)
    begin(1, 1, l)
    rowwise(0, 0, m, mate).start()
    rowwise(0, 1, m, other).start()
    rowwise(1, 0, m, mate).start()
    multiply(2, 1, 2 + late, l, 4, True)
    begin(2, 1, l)
    multiply(0, 1, 3, l, m, True)
    multiply(0, 1, 2, l, l, False)
    begin(0, 1, l)
    middle(2, 0, l)
    middle(2, 0, m)
    middle(2, 1, m)
    middle(1, 1, l)
    finish(1, 1, m)
    rowwise(1, 1, m, other).start()
    middle(2, 1, l)
    middle(0, 1, l)
    finish(2, 0, l)
    finish(2, 0, m)
    rowwise(2, 0, m, mate).start()
    turn(2, 0)
    finish(2, 1, m)
    rowwise(2, 1, m, other).start()
    finish(1, 1, l)
    rowwise(1, 1, l, cross).start()
    turn(1, 1)
    finish(2, 1, l)
    rowwise(2, 1, l, cross).start()
    turn(2, 1)
    finish(0, 1, l)
    rowwise(0, 1, l, cross).start()

    def place(zs, hs, cs, at):
        return pl.ds(pl.multiple_of(zs * 2048 + hs * 1024 + cs * 512 + at, 128), 128)

    for hr in range(2):
        for i in (1, 2):
            for cs in range(2):
                for xs in range(4):
                    remote(
                        turned.at[i - 1, hr, 0, pl.ds(0, 64)], bycol.at[i - 1, hr, cs, xs],
                        st.at[i - 1, hr, 0, 0], rt.at[i - 1, hr, cs, xs], mate,
                    ).wait_recv()
                    out_ref[:, place((z + 4 - i) % 4, (h + hr) % 2, cs, xs * 128)] = bycol[i - 1, hr, cs, xs]
    for i in range(3):
        for cr in range(2):
            byrow[0, l, i, cr] = done[i, 0, cr, pl.ds(pl.multiple_of(l * 64, 64), 64), :]
    low = lax.broadcasted_iota(jnp.int32, (64, 128), 1) < 64
    for hr in range(2):
        for i in range(3):
            if hr == 0:
                rowwise(i, 0, m, mate).wait_send()
                remote(byrow.at[0, m, i], byrow.at[0, m, i], sr.at[i, 0, m], rr.at[i, 0, m], mate).wait_recv()
            else:
                for g in range(2):
                    remote(byrow.at[1, g, i], byrow.at[1, g, i], sr.at[i, 1, g], rr.at[i, 1, g], mate).wait_recv()
            for cr in range(2):
                for t in range(2):
                    v0 = byrow[hr, 0, i, cr, :, t * 128 : t * 128 + 128]
                    v1 = byrow[hr, 1, i, cr, :, t * 128 : t * 128 + 128]
                    even = jnp.where(low, v0, pltpu.roll(v1, 64, 1))
                    odd = jnp.where(low, pltpu.roll(v0, 64, 1), v1)
                    for value, xs in ((even, 2 * t), (odd, 2 * t + 1)):
                        where = place((z + i) % 4, (h + hr) % 2, (c + cr) % 2, xs * 128)
                        if i == 2:
                            out_ref[:, where] += value
                        else:
                            out_ref[:, where] = value

    for one in (mate2, relay2, relay1, other2, down1, down2, far1, core1, core2, core3, core4, core5):
        if one is not mate2 and one is not relay1:
            one.wait_send()
    for i in range(3):
        for hr in range(2):
            for g in range(2):
                for one in scatter1(i, hr, g) + scatter2(i, hr, g):
                    one.wait_send()
                if hr == 1:
                    rowwise(i, 1, g, cross).wait_send()
            if i:
                for one in colwise(i, hr):
                    one.wait_send()


def shards(three_index):
    depth = three_index.shape[0] * three_index.shape[1]
    own = three_index.reshape(depth, 512)
    dma = pltpu.SemaphoreType.DMA
    f32 = jnp.float32
    return pl.pallas_call(
        kernel,
        out_shape=jax.ShapeDtypeStruct((64, 8192), f32),
        in_specs=[pl.BlockSpec(memory_space=pl.ANY)],
        out_specs=pl.BlockSpec(memory_space=pltpu.VMEM),
        scratch_shapes=[
            pltpu.VMEM((depth, 512), jnp.bfloat16),
            pltpu.VMEM((4, 2, depth, 256), jnp.bfloat16),
            pltpu.VMEM((5, 2, depth, 256), jnp.bfloat16),
            pltpu.VMEM((3, 2, 2, 2, 4, 64, 256), f32),
            pltpu.VMEM((3, 2, 2, 2, 2, 64, 256), f32),
            pltpu.VMEM((3, 2, 2, 2, 64, 256), f32),
            pltpu.VMEM((3, 2, 2, 128, 256), f32),
            pltpu.VMEM((2, 2, 2, 256, 128), f32),
            pltpu.VMEM((2, 2, 3, 2, 64, 256), f32),
            pltpu.VMEM((2, 2, 2, 4, 64, 128), f32),
            dma((6,)), dma((14,)), dma((14,)),
            dma((3, 2, 2, 2, 2)), dma((3, 2, 2, 2, 2)), dma((3, 2, 2, 2)), dma((3, 2, 2, 2)),
            dma((3, 2, 2)), dma((3, 2, 2)), dma((2, 2, 2, 4)), dma((2, 2, 2, 4)),
        ],
        compiler_params=pltpu.CompilerParams(
            collective_id=0, has_side_effects=True, vmem_limit_bytes=60 * 2**20
        ),
        cost_estimate=pl.CostEstimate(flops=16 * 10**9, bytes_accessed=8 * 10**6, transcendentals=0),
    )(own)


def solution(mesh):
    return jax.shard_map(
        shards,
        mesh=mesh,
        in_specs=(P("aux", None, "basis"),),
        out_specs=P(("basis", "aux"), None),
        check_vma=False,
    )
```

time: 689 us -> 182 us (0.26)
  waiting for transfers between devices: 615 us -> 0 us
  Pallas kernels: 0 us -> 179 us
  matrix products: 54.8 us -> 0 us
  between operations: 13.4 us -> 0.01 us
    reduce_scatter x1 -> x0, waiting for transfers between devices: 323 us -> none  [shards(): result = lax.psum_scatter(row_block, 'aux', scatter_dimension=0, tiled=True)]
    all_gather x1 -> x0, waiting for transfers between devices: 292 us -> none  [shards(): piece = lax.all_gather(three_index, 'basis', axis=2, tiled=True)]
    pallas_call x0 -> x1, Pallas kernels: none -> 179 us  [shards(): pl.pallas_call(kernel, out_shape=jax.ShapeDtypeStruct((64, 8192), f32), i...]
    dot_general x1 -> x0, matrix products: 54.8 us -> none  [contract(): lax.dot_general(left, right, (((0,), (0,)), ((), ())), preferred_element_...]
  transfers between devices with their start and end apart: 2 -> 0, of which waited for: 2 -> 0; matrix products, arithmetic and copies ran while one was open for 0% -> 0% of each run, Pallas kernels for 0% -> 0%
where the time goes in v1:
time: 182 us
  Pallas kernels  179 us (98%)
  local copies, waits for them, and re-layouts  3.06 us (2%)
    pallas_call x1, Pallas kernels, shards(): pl.pallas_call(kernel, out_shape=jax.ShapeDtypeStruct((64, 8192), f32), i...  179 us

profile of v1, /device:TPU:1, one launch (start us, length us, event | category | flops | bytes accessed | tf_op | source)
XLA Modules:
  0.0 181.7 jit_solution(5551019281876425830)
XLA Ops:
  0.0 178.7 %shard_map.17 = f32[64,8192]{1,0:T(8,128)} custom-call(bf16[3072,512]{1,0:T(8,128)(2,1)} %bitcast.1), custom_call_target="tpu_custom_call" | custom-call | flops 16000000000 | bytes 8000000 | tf_op jit(solution)/shard_map/pallas_call | solution.py:354
  178.7 3.1 %copy.3 = f32[64,8192]{1,0:T(8,128)} copy(f32[64,8192]{1,0:T(8,128)} %shard_map.17) | data formatting | bytes 4194304
